TPU v7x, 256 devices: a whole 4x4x8 slice. The times are simulated.
256 devices in a mesh: brick: 32 (over y_lo, z, core), view: 8 (over y_hi, x).
Axes of the slice: x: 4, y: 4 (y_hi: 2, y_lo: 2; y = y_hi * 2 + y_lo), z: 8, core: 2. Of those that a mesh axis runs over, the one named last changes fastest.
Arguments:
- estimate: float32 [512, 128, 128], P('brick', 'view'), may hold values from 0.5 to 2
- views_data: float32 [8, 512, 128, 128], P('view', 'brick'), may hold values from 0.5 to 2
- psf_taps: float32 [8, 3, 17], P('view'), may hold values from 0.05 to 1
- view_offsets: int32 [8, 2], P('view'), may hold values from -4 to 4
- coverage: int32 [32, 8], P('brick'), may hold values from 0 to 1, as said below
Outputs:
- deconvolved: float32 [512, 128, 128], P('brick', 'view')
Inputs may be any that keep to these rules, and one draw needn't show every extreme that they name: `coverage`: every slab is covered by at least one view.
All inputs are finite; a program needn't handle non-finite values.
Results may differ from a plain program's by a relative error of at most 0.0001.
Values sent between devices are 32-bit elements; how exact they have to be, the bound alone decides.
A program may use at most 64 MiB of HBM per device.

v0:
```python
import jax
import jax.numpy as jnp
from jax import lax
from jax.sharding import PartitionSpec as P

R = 8
ITERS = 4


high = lax.Precision.HIGHEST


def padded_2(block, sides, width):
    for axis, dim in sides:
        count = lax.axis_size(axis)
        forward = [(i, i + 1) for i in range(count - 1)]
        backward = [(target, source) for source, target in forward]
        low = lax.ppermute(
            lax.slice_in_dim(block, block.shape[dim] - width, None, axis=dim), axis, forward
        )
        high = lax.ppermute(lax.slice_in_dim(block, 0, width, axis=dim), axis, backward)
        block = jnp.concatenate([low, block, high], axis=dim)
    return block


def make_band(row, offset, count):
    rows_at = jnp.arange(count, dtype=jnp.int32)[:, None]
    cols_at = jnp.arange(count, dtype=jnp.int32)[None, :]
    index = cols_at - rows_at + offset + R
    taps_at = jnp.arange(row.shape[0], dtype=jnp.int32)
    onehot = index[:, :, None] == taps_at[None, None, :]
    return jnp.sum(jnp.where(onehot, row[None, None, :], 0.0), axis=-1)


def first_band(row, slab_depth, mirror):
    rows_at = jnp.arange(slab_depth, dtype=jnp.int32)[:, None]
    cols_at = jnp.arange(slab_depth + 2 * R, dtype=jnp.int32)[None, :]
    index = 2 * R + rows_at - cols_at if mirror else cols_at - rows_at
    taps_at = jnp.arange(row.shape[0], dtype=jnp.int32)
    onehot = index[:, :, None] == taps_at[None, None, :]
    return jnp.sum(jnp.where(onehot, row[None, None, :], 0.0), axis=-1)


def shards(estimate, views_data, psf_taps, view_offsets, coverage):
    slab_depth = estimate.shape[0]
    cover_row = coverage[0].astype(jnp.float32)
    count = jnp.sum(cover_row)
    current = estimate
    taps = psf_taps[0] / jnp.sum(psf_taps[0], axis=-1, keepdims=True)
    band_y = make_band(taps[1], view_offsets[0, 0], views_data.shape[2])
    band_x = make_band(taps[2], view_offsets[0, 1], views_data.shape[3])
    forward_z = first_band(taps[0], slab_depth, False)
    mirror_z = first_band(taps[0], slab_depth, True)
    mine = jnp.arange(cover_row.shape[0], dtype=jnp.int32) == lax.axis_index("view")
    flag = jnp.sum(jnp.where(mine, cover_row, 0.0))
    recorded = views_data[0]
    for step in range(ITERS):
        whole = lax.all_gather(current, "view", axis=1, tiled=True)
        padded = padded_2(whole, (("brick", 0),), R)
        blurred = jnp.einsum("ip,pyx->iyx", forward_z, padded, precision=high)
        blurred = jnp.einsum("ij,zjx->zix", band_y, blurred, precision=high)
        blurred = jnp.einsum("zyj,ij->zyi", blurred, band_x, precision=high)
        ratio = recorded / blurred
        back = jnp.einsum("zyi,ij->zyj", ratio, band_x, precision=high)
        back = jnp.einsum("ij,zix->zjx", band_y, back, precision=high)
        back_padded = padded_2(back, (("brick", 0),), R)
        back = jnp.einsum("ip,pyx->iyx", mirror_z, back_padded, precision=high)
        weighted = flag * jnp.log(back)
        merged = lax.psum_scatter(weighted, "view", scatter_dimension=1, tiled=True)
        current = current * jnp.exp(merged / count)
    return current


def solution(mesh):
    return jax.shard_map(
        shards,
        mesh=mesh,
        in_specs=(
            P("brick", "view", None),
            P("view", "brick", None, None),
            P("view", None, None),
            P("view", None),
            P("brick", None),
        ),
        out_specs=P("brick", "view", None),
        check_vma=False,
    )
```

profile of v0, /device:TPU:1, one launch (start us, length us, event | category | flops | bytes accessed | tf_op | source)
XLA Modules:
  0.0 714.0 jit_solution(353938572517729823)
XLA Ops:
  6.5 1.6 copy.42
  9.0 1.4 fusion.73
  12.4 53.0 %all-gather.5.cloned.1.call-done = f32[16,128,128]{2,0,1:T(8,128)} async-done(((f32[16,16,128]{2,0,1:T(8,128)}), f32[16,128,128]{2,0,1:T(8,128)}) %all-gather.5.cloned.1.call-update) | async-done | bytes 1048592 | tf_op jit(solution)/shard_map/all_gather | solution.py:58
  65.3 1.4 fusion.72
  66.7 4.6 collective-permute-start
  71.4 1.9 collective-permute-start.1
  73.8 3.7 collective-permute-done
  77.5 4.4 collective-permute-done.1
  83.0 1.9 convolution_bitcast_fusion.7
  84.9 1.8 convolution_divide_fusion.3
  88.9 1.9 collective-permute-start.2
  90.8 2.4 collective-permute-start.3
  93.9 3.0 collective-permute-done.2
  97.7 3.7 collective-permute-done.3
  101.4 1.4 pad_maximum_fusion
  102.8 2.1 copy.41
  104.9 4.4 fusion.27
  110.0 74.5 %reduce-scatter.5.cloned.1.call-done = f32[16,16,128]{2,0,1:T(8,128)} async-done(((f32[16,128,128]{2,0,1:T(8,128)}), f32[16,16,128]{2,0,1:T(8,128)}) %reduce-scatter.5.cloned.1.call-update) | async-done | bytes 131088 | tf_op jit(solution)/shard_map/reduce_scatter | solution.py:69
  184.5 2.2 exponential_multiply_fusion.3
  186.8 53.2 %all-gather.7.cloned.1.call-done = f32[16,128,128]{2,0,1:T(8,128)} async-done(((f32[16,16,128]{2,0,1:T(8,128)}), f32[16,128,128]{2,0,1:T(8,128)}) %all-gather.7.cloned.1.call-update) | async-done | bytes 1048592 | tf_op jit(solution)/shard_map/all_gather | solution.py:58
  241.4 4.6 collective-permute-start.4
  246.0 2.2 collective-permute-start.5
  248.3 3.9 collective-permute-done.4
  252.1 4.5 collective-permute-done.5
  257.8 1.9 convolution_bitcast_fusion.5
  259.7 1.8 convolution_divide_fusion.2
  263.7 1.9 collective-permute-start.6
  265.6 2.4 collective-permute-start.7
  268.1 3.7 collective-permute-done.6
  271.7 4.4 collective-permute-done.7
  276.3 2.1 copy.46
  278.4 4.4 fusion.26
  282.8 75.2 %reduce-scatter.7.cloned.1.call-done = f32[16,16,128]{2,0,1:T(8,128)} async-done(((f32[16,128,128]{2,0,1:T(8,128)}), f32[16,16,128]{2,0,1:T(8,128)}) %reduce-scatter.7.cloned.1.call-update) | async-done | bytes 131088 | tf_op jit(solution)/shard_map/reduce_scatter | solution.py:69
  358.0 2.2 exponential_multiply_fusion.2
  360.3 52.7 %all-gather.9.cloned.1.call-done = f32[16,128,128]{2,0,1:T(8,128)} async-done(((f32[16,16,128]{2,0,1:T(8,128)}), f32[16,128,128]{2,0,1:T(8,128)}) %all-gather.9.cloned.1.call-update) | async-done | bytes 1048592 | tf_op jit(solution)/shard_map/all_gather | solution.py:58
  414.4 4.6 collective-permute-start.8
  419.0 2.3 collective-permute-start.9
  421.3 3.8 collective-permute-done.8
  425.1 4.5 collective-permute-done.9
  430.8 1.9 convolution_bitcast_fusion.3
  432.7 1.8 convolution_divide_fusion.1
  436.7 1.9 collective-permute-start.10
  438.6 2.4 collective-permute-start.11
  441.1 3.7 collective-permute-done.10
  444.7 4.4 collective-permute-done.11
  449.3 2.1 copy.50
  451.4 4.4 fusion.25
  455.8 75.1 %reduce-scatter.9.cloned.1.call-done = f32[16,16,128]{2,0,1:T(8,128)} async-done(((f32[16,128,128]{2,0,1:T(8,128)}), f32[16,16,128]{2,0,1:T(8,128)}) %reduce-scatter.9.cloned.1.call-update) | async-done | bytes 131088 | tf_op jit(solution)/shard_map/reduce_scatter | solution.py:69
  531.0 2.2 exponential_multiply_fusion.1
  533.3 53.2 %all-gather.11.cloned.1.call-done = f32[16,128,128]{2,0,1:T(8,128)} async-done(((f32[16,16,128]{2,0,1:T(8,128)}), f32[16,128,128]{2,0,1:T(8,128)}) %all-gather.11.cloned.1.call-update) | async-done | bytes 1048592 | tf_op jit(solution)/shard_map/all_gather | solution.py:58
  587.8 4.6 collective-permute-start.12
  592.5 2.3 collective-permute-start.13
  594.8 3.8 collective-permute-done.12
  598.6 4.5 collective-permute-done.13
  604.2 1.9 convolution_bitcast_fusion.1
  606.2 1.8 convolution_divide_fusion
  610.1 1.9 collective-permute-start.14
  612.1 2.4 collective-permute-start.15
  614.5 3.7 collective-permute-done.14
  618.2 4.4 collective-permute-done.15
  622.7 2.1 copy.54
  624.8 4.4 fusion.24
  629.2 75.3 %reduce-scatter.11.cloned.1.call-done = f32[16,16,128]{2,0,1:T(8,128)} async-done(((f32[16,128,128]{2,0,1:T(8,128)}), f32[16,16,128]{2,0,1:T(8,128)}) %reduce-scatter.11.cloned.1.call-update) | async-done | bytes 131088 | tf_op jit(solution)/shard_map/reduce_scatter | solution.py:69
  704.5 1.6 exponential_multiply_fusion
  (78 shorter events, 24.0 us)
Async XLA Ops:
  6.5 58.8 %all-gather.5.cloned.1.call-start = ((), (), s32[]{:S(2)}) async-start(), calls=%async_computation.4 | async-start | bytes 1179648 | tf_op jit(solution)/shard_map/all_gather | solution.py:58
  8.2 176.4 %reduce-scatter.5.cloned.1.call-start = ((), (), s32[]{:S(2)}) async-start(), calls=%async_computation.5 | async-start | bytes 1179648 | tf_op jit(solution)/shard_map/reduce_scatter | solution.py:69
  65.3 16.5 %copy-start = (f32[16,128,128]{2,0,1:T(8,128)S(1)}, f32[16,128,128]{2,0,1:T(8,128)}, u32[]{:S(2)}) copy-start(f32[16,128,128]{2,0,1:T(8,128)} %all-gather.5.cloned.1.call-done) | copy-start | bytes 3145732
  66.7 10.8 %collective-permute-start = (f32[8,128,128]{2,0,1:T(8,128)S(1)}, f32[8,128,128]{2,0,1:T(8,128)S(1)}, u32[]{:S(2)}, u32[]{:S(2)}) collective-permute-start(f32[8,128,128]{2,0,1:T(8,128)S(1)} %get-tuple-element.21), channel_id=1, source_target_pairs={{0,8},{8,16},{16,24},{24,32},{32,40},{40,48},{48,56},{56,64},{64,7... | collective-permute-start | bytes 1572872 | tf_op jit(solution)/shard_map/ppermute | solution.py:18
  71.4 10.5 %collective-permute-start.1 = (f32[8,128,128]{2,0,1:T(8,128)S(1)}, f32[8,128,128]{2,0,1:T(8,128)S(1)}, u32[]{:S(2)}, u32[]{:S(2)}) collective-permute-start(f32[8,128,128]{2,0,1:T(8,128)S(1)} %get-tuple-element.22), channel_id=1, source_target_pairs={{8,0},{16,8},{24,16},{32,24},{40,32},{48,40},{56,48},{64,56},{72,6... | collective-permute-start | bytes 1572872 | tf_op jit(solution)/shard_map/ppermute | solution.py:21
  81.9 3.0 copy-start.9
  87.8 5.5 copy-start.13
  88.9 8.0 %collective-permute-start.2 = (f32[8,128,128]{1,2,0:T(8,128)S(1)}, f32[8,128,128]{1,2,0:T(8,128)S(1)}, u32[]{:S(2)}, u32[]{:S(2)}) collective-permute-start(f32[8,128,128]{1,2,0:T(8,128)S(1)} %get-tuple-element.19), channel_id=1, source_target_pairs={{0,8},{8,16},{16,24},{24,32},{32,40},{40,48},{48,56},{56,64},{64,7... | collective-permute-start | bytes 1572872 | tf_op jit(solution)/shard_map/ppermute | solution.py:18
  90.8 10.6 %collective-permute-start.3 = (f32[8,128,128]{1,2,0:T(8,128)S(1)}, f32[8,128,128]{1,2,0:T(8,128)}, u32[]{:S(2)}, u32[]{:S(2)}) collective-permute-start(f32[8,128,128]{1,2,0:T(8,128)S(1)} %get-tuple-element.20), channel_id=1, source_target_pairs={{8,0},{16,8},{24,16},{32,24},{40,32},{48,40},{56,48},{64,56},{72,6... | collective-permute-start | bytes 1572872 | tf_op jit(solution)/shard_map/ppermute | solution.py:21
  96.9 0.8 copy-start.8
  104.9 79.6 %copy-start.7 = (f32[16,16,128]{2,1,0:T(8,128)S(1)}, f32[16,16,128]{2,1,0:T(8,128)}, u32[]{:S(2)}) copy-start(f32[16,16,128]{2,1,0:T(8,128)} %param.5) | copy-start | bytes 393220
  109.3 130.7 %all-gather.7.cloned.1.call-start = ((), (), s32[]{:S(2)}) async-start(), calls=%async_computation.6 | async-start | bytes 1179648 | tf_op jit(solution)/shard_map/all_gather | solution.py:58
  186.8 171.2 %reduce-scatter.7.cloned.1.call-start = ((), (), s32[]{:S(2)}) async-start(), calls=%async_computation.7 | async-start | bytes 1179648 | tf_op jit(solution)/shard_map/reduce_scatter | solution.py:69
  240.0 16.7 %copy-start.2 = (f32[16,128,128]{2,0,1:T(8,128)S(1)}, f32[16,128,128]{2,0,1:T(8,128)}, u32[]{:S(2)}) copy-start(f32[16,128,128]{2,0,1:T(8,128)} %all-gather.7.cloned.1.call-done) | copy-start | bytes 3145732
  241.4 10.8 %collective-permute-start.4 = (f32[8,128,128]{2,0,1:T(8,128)S(1)}, f32[8,128,128]{2,0,1:T(8,128)S(1)}, u32[]{:S(2)}, u32[]{:S(2)}) collective-permute-start(f32[8,128,128]{2,0,1:T(8,128)S(1)} %get-tuple-element.17), channel_id=1, source_target_pairs={{0,8},{8,16},{16,24},{24,32},{32,40},{40,48},{48,56},{56,64},{64,7... | collective-permute-start | bytes 1572872 | tf_op jit(solution)/shard_map/ppermute | solution.py:18
  246.0 13.7 %copy-start.10 = (f32[1,16,128,128]{3,2,1,0:T(8,128)S(1)}, f32[1,16,128,128]{3,2,1,0:T(8,128)}, u32[]{:S(2)}) copy-start(f32[1,16,128,128]{3,2,1,0:T(8,128)} %param.6) | copy-start | bytes 3145732
  246.0 10.6 %collective-permute-start.5 = (f32[8,128,128]{2,0,1:T(8,128)S(1)}, f32[8,128,128]{2,0,1:T(8,128)S(1)}, u32[]{:S(2)}, u32[]{:S(2)}) collective-permute-start(f32[8,128,128]{2,0,1:T(8,128)S(1)} %get-tuple-element.18), channel_id=1, source_target_pairs={{8,0},{16,8},{24,16},{32,24},{40,32},{48,40},{56,48},{64,56},{72,6... | collective-permute-start | bytes 1572872 | tf_op jit(solution)/shard_map/ppermute | solution.py:21
  263.7 8.0 %collective-permute-start.6 = (f32[8,128,128]{1,2,0:T(8,128)S(1)}, f32[8,128,128]{1,2,0:T(8,128)S(1)}, u32[]{:S(2)}, u32[]{:S(2)}) collective-permute-start(f32[8,128,128]{1,2,0:T(8,128)S(1)} %get-tuple-element.15), channel_id=1, source_target_pairs={{0,8},{8,16},{16,24},{24,32},{32,40},{40,48},{48,56},{56,64},{64,7... | collective-permute-start | bytes 1572872 | tf_op jit(solution)/shard_map/ppermute | solution.py:18
  265.6 10.5 %collective-permute-start.7 = (f32[8,128,128]{1,2,0:T(8,128)S(1)}, f32[8,128,128]{1,2,0:T(8,128)S(1)}, u32[]{:S(2)}, u32[]{:S(2)}) collective-permute-start(f32[8,128,128]{1,2,0:T(8,128)S(1)} %get-tuple-element.16), channel_id=1, source_target_pairs={{8,0},{16,8},{24,16},{32,24},{40,32},{48,40},{56,48},{64,56},{72,6... | collective-permute-start | bytes 1572872 | tf_op jit(solution)/shard_map/ppermute | solution.py:21
  278.4 79.7 %copy-start.6 = (f32[16,16,128]{2,0,1:T(8,128)S(1)}, f32[16,16,128]{2,0,1:T(8,128)}, u32[]{:S(2)}) copy-start(f32[16,16,128]{2,0,1:T(8,128)} %exponential_multiply_fusion.3) | copy-start | bytes 393220
  282.8 130.2 %all-gather.9.cloned.1.call-start = ((), (), s32[]{:S(2)}) async-start(), calls=%async_computation.8 | async-start | bytes 1179648 | tf_op jit(solution)/shard_map/all_gather | solution.py:58
  360.2 170.7 %reduce-scatter.9.cloned.1.call-start = ((), (), s32[]{:S(2)}) async-start(), calls=%async_computation.9 | async-start | bytes 1179648 | tf_op jit(solution)/shard_map/reduce_scatter | solution.py:69
  413.0 16.7 %copy-start.3 = (f32[16,128,128]{2,0,1:T(8,128)S(1)}, f32[16,128,128]{2,0,1:T(8,128)}, u32[]{:S(2)}) copy-start(f32[16,128,128]{2,0,1:T(8,128)} %all-gather.9.cloned.1.call-done) | copy-start | bytes 3145732
  414.4 10.8 %collective-permute-start.8 = (f32[8,128,128]{2,0,1:T(8,128)S(1)}, f32[8,128,128]{2,0,1:T(8,128)S(1)}, u32[]{:S(2)}, u32[]{:S(2)}) collective-permute-start(f32[8,128,128]{2,0,1:T(8,128)S(1)} %get-tuple-element.13), channel_id=1, source_target_pairs={{0,8},{8,16},{16,24},{24,32},{32,40},{40,48},{48,56},{56,64},{64,7... | collective-permute-start | bytes 1572872 | tf_op jit(solution)/shard_map/ppermute | solution.py:18
  419.0 13.7 %copy-start.11 = (f32[1,16,128,128]{3,2,1,0:T(8,128)S(1)}, f32[1,16,128,128]{3,2,1,0:T(8,128)}, u32[]{:S(2)}) copy-start(f32[1,16,128,128]{3,2,1,0:T(8,128)} %param.6) | copy-start | bytes 3145732
  419.0 10.6 %collective-permute-start.9 = (f32[8,128,128]{2,0,1:T(8,128)S(1)}, f32[8,128,128]{2,0,1:T(8,128)S(1)}, u32[]{:S(2)}, u32[]{:S(2)}) collective-permute-start(f32[8,128,128]{2,0,1:T(8,128)S(1)} %get-tuple-element.14), channel_id=1, source_target_pairs={{8,0},{16,8},{24,16},{32,24},{40,32},{48,40},{56,48},{64,56},{72,6... | collective-permute-start | bytes 1572872 | tf_op jit(solution)/shard_map/ppermute | solution.py:21
  436.7 8.0 %collective-permute-start.10 = (f32[8,128,128]{1,2,0:T(8,128)S(1)}, f32[8,128,128]{1,2,0:T(8,128)S(1)}, u32[]{:S(2)}, u32[]{:S(2)}) collective-permute-start(f32[8,128,128]{1,2,0:T(8,128)S(1)} %get-tuple-element.11), channel_id=1, source_target_pairs={{0,8},{8,16},{16,24},{24,32},{32,40},{40,48},{48,56},{56,64},{64,7... | collective-permute-start | bytes 1572872 | tf_op jit(solution)/shard_map/ppermute | solution.py:18
  438.6 10.5 %collective-permute-start.11 = (f32[8,128,128]{1,2,0:T(8,128)S(1)}, f32[8,128,128]{1,2,0:T(8,128)S(1)}, u32[]{:S(2)}, u32[]{:S(2)}) collective-permute-start(f32[8,128,128]{1,2,0:T(8,128)S(1)} %get-tuple-element.12), channel_id=1, source_target_pairs={{8,0},{16,8},{24,16},{32,24},{40,32},{48,40},{56,48},{64,56},{72,6... | collective-permute-start | bytes 1572872 | tf_op jit(solution)/shard_map/ppermute | solution.py:21
  451.4 79.6 %copy-start.5 = (f32[16,16,128]{2,0,1:T(8,128)S(1)}, f32[16,16,128]{2,0,1:T(8,128)}, u32[]{:S(2)}) copy-start(f32[16,16,128]{2,0,1:T(8,128)} %exponential_multiply_fusion.2) | copy-start | bytes 393220
  455.8 130.7 %all-gather.11.cloned.1.call-start = ((), (), s32[]{:S(2)}) async-start(), calls=%async_computation.10 | async-start | bytes 1179648 | tf_op jit(solution)/shard_map/all_gather | solution.py:58
  533.2 171.2 %reduce-scatter.11.cloned.1.call-start = ((), (), s32[]{:S(2)}) async-start(), calls=%async_computation.11 | async-start | bytes 1179648 | tf_op jit(solution)/shard_map/reduce_scatter | solution.py:69
  586.4 16.7 %copy-start.1 = (f32[16,128,128]{2,0,1:T(8,128)S(1)}, f32[16,128,128]{2,0,1:T(8,128)}, u32[]{:S(2)}) copy-start(f32[16,128,128]{2,0,1:T(8,128)} %all-gather.11.cloned.1.call-done) | copy-start | bytes 3145732
  587.8 10.8 %collective-permute-start.12 = (f32[8,128,128]{2,0,1:T(8,128)S(1)}, f32[8,128,128]{2,0,1:T(8,128)S(1)}, u32[]{:S(2)}, u32[]{:S(2)}) collective-permute-start(f32[8,128,128]{2,0,1:T(8,128)S(1)} %get-tuple-element.9), channel_id=1, source_target_pairs={{0,8},{8,16},{16,24},{24,32},{32,40},{40,48},{48,56},{56,64},{64,7... | collective-permute-start | bytes 1572872 | tf_op jit(solution)/shard_map/ppermute | solution.py:18
  592.5 13.7 %copy-start.12 = (f32[1,16,128,128]{3,2,1,0:T(8,128)S(1)}, f32[1,16,128,128]{3,2,1,0:T(8,128)}, u32[]{:S(2)}) copy-start(f32[1,16,128,128]{3,2,1,0:T(8,128)} %param.6) | copy-start | bytes 3145732
  592.5 10.6 %collective-permute-start.13 = (f32[8,128,128]{2,0,1:T(8,128)S(1)}, f32[8,128,128]{2,0,1:T(8,128)S(1)}, u32[]{:S(2)}, u32[]{:S(2)}) collective-permute-start(f32[8,128,128]{2,0,1:T(8,128)S(1)} %get-tuple-element.10), channel_id=1, source_target_pairs={{8,0},{16,8},{24,16},{32,24},{40,32},{48,40},{56,48},{64,56},{72,6... | collective-permute-start | bytes 1572872 | tf_op jit(solution)/shard_map/ppermute | solution.py:21
  610.1 8.0 %collective-permute-start.14 = (f32[8,128,128]{1,2,0:T(8,128)S(1)}, f32[8,128,128]{1,2,0:T(8,128)S(1)}, u32[]{:S(2)}, u32[]{:S(2)}) collective-permute-start(f32[8,128,128]{1,2,0:T(8,128)S(1)} %get-tuple-element.7), channel_id=1, source_target_pairs={{0,8},{8,16},{16,24},{24,32},{32,40},{40,48},{48,56},{56,64},{64,7... | collective-permute-start | bytes 1572872 | tf_op jit(solution)/shard_map/ppermute | solution.py:18
  612.1 10.5 %collective-permute-start.15 = (f32[8,128,128]{1,2,0:T(8,128)S(1)}, f32[8,128,128]{1,2,0:T(8,128)S(1)}, u32[]{:S(2)}, u32[]{:S(2)}) collective-permute-start(f32[8,128,128]{1,2,0:T(8,128)S(1)} %get-tuple-element.8), channel_id=1, source_target_pairs={{8,0},{16,8},{24,16},{32,24},{40,32},{48,40},{56,48},{64,56},{72,6... | collective-permute-start | bytes 1572872 | tf_op jit(solution)/shard_map/ppermute | solution.py:21
  624.8 79.7 %copy-start.4 = (f32[16,16,128]{2,0,1:T(8,128)S(1)}, f32[16,16,128]{2,0,1:T(8,128)}, u32[]{:S(2)}) copy-start(f32[16,16,128]{2,0,1:T(8,128)} %exponential_multiply_fusion.1) | copy-start | bytes 393220
Sparse Core Ops, SparseCore 0:
  10.0 55.3 all-gather.4
  109.5 75.0 reduce-scatter.4
  187.5 52.4 all-gather.6
  282.9 75.0 reduce-scatter.6
  360.5 52.4 all-gather.8
  455.9 75.0 reduce-scatter.8
  533.9 52.4 all-gather.10
  629.3 75.0 reduce-scatter.10
where the time goes:
time: 723 us; the launch traced here: 714 us
  waiting for transfers between devices  576 us (80%)
  matrix products  45.1 us (6%)
  starting transfers between devices  45 us (6%)
  local copies, waits for them, and re-layouts  18.6 us (3%)
  other arithmetic  14.5 us (2%)
  between operations  14.4 us (2%)
    reduce_scatter x4, waiting for transfers between devices, shards(): merged = lax.psum_scatter(weighted, 'view', scatter_dimension=1, tiled=True)  300 us
    all_gather x4, waiting for transfers between devices, shards(): whole = lax.all_gather(current, 'view', axis=1, tiled=True)  212 us
    ppermute x8, waiting for transfers between devices, padded_2(): lax.ppermute(lax.slice_in_dim(block, 0, width, axis=dim), axis, backward)  34.9 us
    ppermute x8, waiting for transfers between devices, padded_2(): lax.ppermute(lax.slice_in_dim(block, block.shape[dim] - width, None, axis...  29.2 us
    ppermute x8, starting transfers between devices, padded_2(): lax.ppermute(lax.slice_in_dim(block, block.shape[dim] - width, None, axis...  26.3 us
    ppermute x8, starting transfers between devices, padded_2(): lax.ppermute(lax.slice_in_dim(block, 0, width, axis=dim), axis, backward)  18.5 us
    dot_general x4, matrix products, shards(): back = jnp.einsum('ip,pyx->iyx', mirror_z, back_padded, precision=high)  17.5 us
  transfers between devices with their start and end apart: 24, of which 24 were waited for; matrix products, arithmetic and copies ran while one was open for 1% of the time, Pallas kernels for 0%

commit v1 on v0

v1 whole, which is shorter than its diff:
```python
import functools

import jax
import jax.numpy as jnp
from jax import lax
from jax.experimental import pallas as pl
from jax.experimental.pallas import tpu as pltpu
from jax.sharding import PartitionSpec as P

R = 8
KW = 2 * R + 1
ITERS = 4
XS = 4
MESH = pl.DeviceIdType.MESH
BF16 = jnp.bfloat16
F32 = jnp.float32


def split(value):
    upper = value.astype(BF16)
    return upper, (value - upper.astype(F32)).astype(BF16)


def kernel(
    bricks, views, est_ref, rec_ref, taps_ref, off_ref, cov_ref, out_ref,
    own, whole, blur, back, logs, sums, fy, fx, gy, gx,
    ag_send, ag_recv, hp_send, hn_send, hp_recv, hn_recv,
    bp_send, bn_send, bp_recv, bn_recv, rs_send, rs_recv,
):
    slab, piece, width = est_ref.shape
    rows = piece * views
    brick, view = lax.axis_index("brick"), lax.axis_index("view")
    half = views // XS

    def peer(k, sign):
        dx, dy = k % XS, k // XS
        x = lax.rem(view % XS + sign * dx + XS, XS)
        y = lax.rem(view // XS + sign * dy + half, half)
        return y * XS + x

    has_prev, has_next = brick > 0, brick < bricks - 1

    barrier = pltpu.get_barrier_semaphore()
    for k in range(1, views):
        pl.semaphore_signal(barrier, inc=1, device_id=(brick, peer(k, 1)), device_id_type=MESH)

    @pl.when(has_prev)
    def _():
        pl.semaphore_signal(barrier, inc=1, device_id=(brick - 1, view), device_id_type=MESH)

    @pl.when(has_next)
    def _():
        pl.semaphore_signal(barrier, inc=1, device_id=(brick + 1, view), device_id_type=MESH)

    def total(row):
        value = taps_ref[0, row, 0]
        for k in range(1, KW):
            value = value + taps_ref[0, row, k]
        return value

    def fill(row, offset, scale, lhs, rhs_up, ref):
        r = lax.broadcasted_iota(jnp.int32, (rows, rows), 0)
        c = lax.broadcasted_iota(jnp.int32, (rows, rows), 1)
        index = (c - r if rhs_up else r - c) + offset + R
        band = jnp.zeros((rows, rows), F32)
        for k in range(KW):
            band = jnp.where(index == k, taps_ref[0, row, k], band)
        upper, lower = split(band / jnp.full((rows, rows), scale, F32))
        if lhs:
            ref[...] = jnp.concatenate(
                [jnp.concatenate([upper, upper], 1), jnp.concatenate([lower, lower], 1)], 0)
        else:
            ref[...] = jnp.concatenate(
                [jnp.concatenate([upper, lower], 1), jnp.concatenate([upper, lower], 1)], 0)

    scale_y = total(1)
    scale_x = total(2) * total(0)
    fill(1, off_ref[0, 0], scale_y, True, True, fy)
    fill(1, off_ref[0, 0], scale_y, True, False, gy)
    fill(2, off_ref[0, 1], scale_x, False, False, fx)
    fill(2, off_ref[0, 1], scale_x, False, True, gx)

    count = cov_ref[0, 0]
    for k in range(1, views):
        count = count + cov_ref[0, k]
    count = count.astype(F32)
    flag = cov_ref[0, view].astype(F32)

    @pl.when(jnp.logical_not(has_prev))
    def _():
        whole[0:R] = jnp.zeros((R, rows, width), F32)
        back[0:R] = jnp.zeros((R, rows, width), F32)

    @pl.when(jnp.logical_not(has_next))
    def _():
        whole[R + slab:] = jnp.zeros((R, rows, width), F32)
        back[R + slab:] = jnp.zeros((R, rows, width), F32)

    def at(owner):
        return pl.ds(pl.multiple_of(owner * piece, piece), piece)

    def gather(k):
        return pltpu.make_async_remote_copy(
            own, whole.at[pl.ds(R, slab), at(view)], ag_send.at[k], ag_recv.at[k],
            device_id=(brick, peer(k, 1)), device_id_type=MESH)

    def to_prev(buf, k, owner, send, recv):
        return pltpu.make_async_remote_copy(
            buf.at[pl.ds(R, R), at(owner)], buf.at[pl.ds(R + slab, R), at(owner)],
            send.at[k], recv.at[k], device_id=(brick - 1, view), device_id_type=MESH)

    def to_next(buf, k, owner, send, recv):
        return pltpu.make_async_remote_copy(
            buf.at[pl.ds(slab, R), at(owner)], buf.at[pl.ds(0, R), at(owner)],
            send.at[k], recv.at[k], device_id=(brick + 1, view), device_id_type=MESH)

    def scatter(k):
        return pltpu.make_async_remote_copy(
            logs.at[:, at(peer(k, 1))], sums.at[k], rs_send.at[k], rs_recv.at[k],
            device_id=(brick, peer(k, 1)), device_id_type=MESH)

    def convolve(buf, owner, mirror, store):
        def tile(i, carry):
            place = pl.ds(pl.multiple_of(owner * piece + i * 8, 8), 8)
            layers = [buf[z, place, :] for z in range(slab + 2 * R)]
            for z in range(slab):
                acc = None
                for k in range(KW):
                    term = taps_ref[0, 0, k] * layers[z + 2 * R - k if mirror else z + k]
                    acc = term if acc is None else acc + term
                store(z, place, i, acc)
            return carry
        lax.fori_loop(0, piece // 8, tile, 0)

    def store_blur(z, place, i, value):
        blur[z, place, :] = value

    def store_logs(z, place, i, value):
        logs[z, place, :] = flag * jnp.log(value)

    def store_own(z, place, i, value):
        sums[0, z, pl.ds(pl.multiple_of(i * 8, 8), 8), :] = flag * jnp.log(value)

    def bands(z):
        h0, l0 = split(blur[z])
        h1, l1 = split(blur[z + 1])
        data = jnp.concatenate([jnp.concatenate([h0, h1], 1), jnp.concatenate([l0, l1], 1)], 0)
        o = jnp.dot(fy[...], data, preferred_element_type=F32)
        o = o[:rows] + o[rows:]
        h, l = split(jnp.concatenate([o[:, :width], o[:, width:]], 0))
        o = jnp.dot(jnp.concatenate([h, l], 1), fx[...], preferred_element_type=F32)
        o = o[:, :width] + o[:, width:]
        recorded = jnp.concatenate([rec_ref[0, z], rec_ref[0, z + 1]], 0)
        h, l = split(recorded / o)
        o = jnp.dot(jnp.concatenate([h, l], 1), gx[...], preferred_element_type=F32)
        h, l = split(o[:, :width] + o[:, width:])
        data = jnp.concatenate(
            [jnp.concatenate([h[:rows], h[rows:]], 1), jnp.concatenate([l[:rows], l[rows:]], 1)], 0)
        o = jnp.dot(gy[...], data, preferred_element_type=F32)
        o = o[:rows] + o[rows:]
        back[R + z] = o[:, :width]
        back[R + z + 1] = o[:, width:]

    def half_bands(start):
        def pair(i, carry):
            for j in range(2):
                bands(start + 4 * i + 2 * j)
            return carry
        lax.fori_loop(0, R // 4, pair, 0)

    own[...] = est_ref[...]
    partners = views - 1 + has_prev.astype(jnp.int32) + has_next.astype(jnp.int32)
    pl.semaphore_wait(barrier, partners)

    def each(first, last, body):
        def step(k, carry):
            body(k)
            return carry
        lax.fori_loop(first, last, step, 0)

    each(1, views, lambda k: gather(k).start())

    def iteration(t, carry):
        whole[pl.ds(R, slab), at(view)] = own[...]

        def arrive(k):
            owner = peer(k, -1)

            @pl.when(k > 0)
            def _():
                gather(k).wait_recv()

            @pl.when(has_prev)
            def _():
                to_prev(whole, k, owner, hp_send, hn_recv).start()

            @pl.when(has_next)
            def _():
                to_next(whole, k, owner, hn_send, hp_recv).start()

        each(0, views, arrive)

        def forward(k):
            owner = peer(k, -1)

            @pl.when(has_next)
            def _():
                to_prev(whole, k, owner, hp_send, hn_recv).wait_recv()

            @pl.when(has_prev)
            def _():
                to_next(whole, k, owner, hn_send, hp_recv).wait_recv()
            convolve(whole, owner, False, store_blur)

        each(0, views, forward)

        def sent(k):
            owner = peer(k, -1)

            @pl.when(has_prev)
            def _():
                to_prev(whole, k, owner, hp_send, hn_recv).wait_send()

            @pl.when(has_next)
            def _():
                to_next(whole, k, owner, hn_send, hp_recv).wait_send()

        each(0, views, sent)
        each(1, views, lambda k: gather(k).wait_send())

        half_bands(0)

        @pl.when(has_prev)
        def _():
            each(1, views, lambda k: to_prev(back, k, peer(k, 1), bp_send, bn_recv).start())
            to_prev(back, 0, view, bp_send, bn_recv).start()
        half_bands(R)

        @pl.when(has_next)
        def _():
            each(1, views, lambda k: to_next(back, k, peer(k, 1), bn_send, bp_recv).start())
            to_next(back, 0, view, bn_send, bp_recv).start()

        def backward(k):
            owner = peer(k, 1)

            @pl.when(has_next)
            def _():
                to_prev(back, k, owner, bp_send, bn_recv).wait_recv()

            @pl.when(has_prev)
            def _():
                to_next(back, k, owner, bn_send, bp_recv).wait_recv()

        def backward_peer(k):
            backward(k)
            convolve(back, peer(k, 1), True, store_logs)
            scatter(k).start()

        each(1, views, backward_peer)
        backward(0)
        convolve(back, view, True, store_own)
        each(1, views, lambda k: scatter(k).wait_recv())
        merged = sums[0]
        for k in range(1, views):
            merged = merged + sums[k]
        own[...] = own[...] * jnp.exp(merged / jnp.full(merged.shape, count, F32))

        @pl.when(t < ITERS - 1)
        def _():
            each(1, views, lambda k: gather(k).start())

        each(1, views, lambda k: scatter(k).wait_send())

        def back_sent(k):
            @pl.when(has_prev)
            def _():
                to_prev(back, k, peer(k, 1), bp_send, bn_recv).wait_send()

            @pl.when(has_next)
            def _():
                to_next(back, k, peer(k, 1), bn_send, bp_recv).wait_send()

        each(0, views, back_sent)
        return carry

    lax.fori_loop(0, ITERS, iteration, 0)
    out_ref[...] = own[...]


def shards(bricks, views, estimate, views_data, psf_taps, view_offsets, coverage):
    slab, piece, width = estimate.shape
    rows = piece * views
    dma = pltpu.SemaphoreType.DMA((views,))
    return pl.pallas_call(
        functools.partial(kernel, bricks, views),
        out_shape=jax.ShapeDtypeStruct(estimate.shape, F32),
        in_specs=[pl.BlockSpec(memory_space=pltpu.VMEM)] * 2 + [pl.BlockSpec(memory_space=pltpu.SMEM)] * 3,
        out_specs=pl.BlockSpec(memory_space=pltpu.VMEM),
        scratch_shapes=[
            pltpu.VMEM((slab, piece, width), F32),
            pltpu.VMEM((slab + 2 * R, rows, width), F32),
            pltpu.VMEM((slab, rows, width), F32),
            pltpu.VMEM((slab + 2 * R, rows, width), F32),
            pltpu.VMEM((slab, rows, width), F32),
            pltpu.VMEM((views, slab, piece, width), F32),
        ] + [pltpu.VMEM((2 * rows, 2 * rows), BF16)] * 4 + [dma] * 12,
        compiler_params=pltpu.CompilerParams(
            collective_id=0, has_side_effects=True, vmem_limit_bytes=40 << 20),
        name="deconvolve",
    )(estimate, views_data, psf_taps, view_offsets, coverage)


def solution(mesh):
    return jax.shard_map(
        functools.partial(shards, mesh.shape["brick"], mesh.shape["view"]),
        mesh=mesh,
        in_specs=(
            P("brick", "view", None),
            P("view", "brick", None, None),
            P("view", None, None),
            P("view", None),
            P("brick", None),
        ),
        out_specs=P("brick", "view", None),
        check_vma=False,
    )
```

time: 723 us -> 199 us (0.28)
  the two profiles are of different devices: /device:TPU:1 before, /device:TPU:248 now
where the time goes in v1:
time: 199 us
  Pallas kernels  195 us (98%)
  local copies, waits for them, and re-layouts  3.5 us (2%)
    pallas_call x1, Pallas kernels, shards(): pl.pallas_call(functools.partial(kernel, bricks, views), out_shape=jax.Sh...  195 us

profile of v1, /device:TPU:248, one launch (start us, length us, event | category | flops | bytes accessed | tf_op | source)
XLA Modules:
  0.0 198.6 jit_solution(12110889594738557259)
XLA Ops:
  0.0 0.0 copy-start.3
  0.0 0.0 copy-start.2
  0.0 0.7 copy.6.taps_ref
  0.7 0.0 copy-done.3
  0.7 0.0 copy-done.2
  0.7 0.0 copy-start
  0.7 1.2 copy-done
  1.9 0.0 copy-start.1
  1.9 0.9 copy-done.1
  2.9 195.1 %deconvolve.1 = f32[16,16,128]{2,1,0:T(8,128)S(1)} custom-call(f32[16,16,128]{2,1,0:T(8,128)S(1)} %copy-done.1, f32[1,16,128,128]{3,2,1,0:T(8,128)S(1)} %copy-done, f32[1,3,17]{2,1,0:T(4,128)S(1)} %copy.6.taps_ref, s32[1,2]{1,0:T(1,128)S(1)} %copy-done.2, s32[1,8]{1,0:T(1,128)S(1)} %copy-done.3), custom_call_target="tpu_custom_call" | custom-call | tf_op jit(solution)/shard_map/deconvolve/pallas_call | solution.py:295
  198.0 0.7 copy.8
Async XLA Ops:
  0.0 0.7 copy-start.3
  0.0 0.7 copy-start.2
  0.7 1.2 copy-start
  1.9 0.9 copy-start.1

commit v2 on v0

v2 whole, which is shorter than its diff:
```python
import functools

import jax
import jax.numpy as jnp
from jax import lax
from jax.experimental import pallas as pl
from jax.experimental.pallas import tpu as pltpu
from jax.sharding import PartitionSpec as P

R = 8
KW = 2 * R + 1
ITERS = 4
XS = 4
ORDER = (0, 1)
LAG = 5
GATHER_BY = True
SCATTER_BY = True
GROUP = 4
MESH = pl.DeviceIdType.MESH
BF16 = jnp.bfloat16
F32 = jnp.float32


def split(value):
    upper = value.astype(BF16)
    return upper, (value - upper.astype(F32)).astype(BF16)


def kernel(
    bricks, views, est_ref, rec_hbm, taps_ref, off_ref, cov_ref, out_ref,
    rec_ref, own, whole, blur, back, logs, sums, conv, fy, fx, gy, gx,
    ag_send, ag_recv, est_send, est_recv, back_send, back_recv, rs_send, rs_recv, rec_sem,
):
    slab, piece, width = est_ref.shape
    rows = piece * views
    brick, view = lax.axis_index("brick"), lax.axis_index("view")
    half = views // XS
    core = brick % 2
    first, second = ORDER

    def peer(k, sign):
        dx, dy = k % XS, k // XS
        x = lax.rem(view % XS + sign * dx + XS, XS)
        y = lax.rem(view // XS + sign * dy + half, half)
        return y * XS + x

    begin = (R * core, R * (1 - core))
    beside = tuple(brick + start // (R // 2) - 1 for start in begin)
    exists = (jnp.logical_and(beside[0] >= 0, beside[0] < bricks), None)

    def guarded(i, body):
        if exists[i] is None:
            body()
        else:
            pl.when(exists[i])(body)

    def each(first, last, body):
        def step(k, carry):
            body(k)
            return carry
        lax.fori_loop(first, last, step, 0)

    barrier = pltpu.get_barrier_semaphore()

    def greet(target):
        pl.semaphore_signal(barrier, inc=1, device_id=target, device_id_type=MESH)

    each(1, views, lambda k: greet((brick, peer(k, 1))))
    for i in range(2):
        guarded(i, lambda: greet((beside[i], view)))

    record = pltpu.make_async_copy(rec_hbm.at[0], rec_ref, rec_sem)
    record.start()
    own[...] = est_ref[...]
    pl.semaphore_wait(barrier, views + exists[0].astype(jnp.int32))

    def at(owner):
        return pl.ds(pl.multiple_of(owner * piece, piece), piece)

    def gather(i, k):
        return pltpu.make_async_remote_copy(
            own.at[pl.ds(begin[i], R)], whole.at[pl.ds(R + begin[i], R), at(view)],
            ag_send.at[i, k], ag_recv.at[i, k], device_id=(brick, peer(k, 1)), device_id_type=MESH)

    def halo(buf, i, k, owner, send, recv):
        return pltpu.make_async_remote_copy(
            buf.at[pl.ds(R + begin[i], R), at(owner)], buf.at[pl.ds(R + slab - 3 * begin[i], R), at(owner)],
            send.at[i, k], recv.at[i, k], device_id=(beside[i], view), device_id_type=MESH)

    def est_halo(i, k):
        return halo(whole, i, k, peer(k, -1), est_send, est_recv)

    def back_halo(i, k):
        return halo(back, i, k, peer(k, 1), back_send, back_recv)

    def relay(k):
        place = whole.at[pl.ds(R + begin[first], R), at(peer(XS, 1))]
        return pltpu.make_async_remote_copy(
            place, place, ag_send.at[first, k], ag_recv.at[first, k],
            device_id=(brick, peer(k - XS, 1)), device_id_type=MESH)

    def scatter(i, k, target):
        return pltpu.make_async_remote_copy(
            logs.at[pl.ds(begin[i], R), at(peer(k, 1))], sums.at[i, k], rs_send.at[i, k], rs_recv.at[i, k],
            device_id=(brick, peer(target, 1)), device_id_type=MESH)

    def send_own(i):
        if GATHER_BY and i == first:
            each(1, XS + 1, lambda k: gather(i, XS + 1 - k).start())
        else:
            each(1, views, lambda k: gather(i, turn(k, 2)).start())

    def turn(k, shift):
        return (k + shift) % (views - 1) + 1

    for i in ORDER:
        send_own(i)

    def total(row):
        value = taps_ref[0, row, 0]
        for k in range(1, KW):
            value = value + taps_ref[0, row, k]
        return value

    def fill(row, offset, scale, lhs, rhs_up, ref):
        r = lax.broadcasted_iota(jnp.int32, (rows, rows), 0)
        c = lax.broadcasted_iota(jnp.int32, (rows, rows), 1)
        index = (c - r if rhs_up else r - c) + offset + R
        band = jnp.zeros((rows, rows), F32)
        for k in range(KW):
            band = jnp.where(index == k, taps_ref[0, row, k], band)
        upper, lower = split(band / jnp.full((rows, rows), scale, F32))
        if lhs:
            ref[...] = jnp.concatenate(
                [jnp.concatenate([upper, upper], 1), jnp.concatenate([lower, lower], 1)], 0)
        else:
            ref[...] = jnp.concatenate(
                [jnp.concatenate([upper, lower], 1), jnp.concatenate([upper, lower], 1)], 0)

    scale_y = total(1)
    scale_x = total(2) * total(0)
    fill(1, off_ref[0, 0], scale_y, True, True, fy)
    fill(1, off_ref[0, 0], scale_y, True, False, gy)
    fill(2, off_ref[0, 1], scale_x, False, False, fx)
    fill(2, off_ref[0, 1], scale_x, False, True, gx)

    count = cov_ref[0, 0]
    for k in range(1, views):
        count = count + cov_ref[0, k]
    count = count.astype(F32)
    flag = cov_ref[0, view].astype(F32)

    @pl.when(jnp.logical_not(exists[0]))
    def _():
        edge = pl.ds(R + slab - 3 * begin[1], R)
        whole[edge] = jnp.zeros((R, rows, width), F32)
        back[edge] = jnp.zeros((R, rows, width), F32)

    def convolve(buf, owner, start, layers, mirror, store):
        def tile(i, carry):
            place = pl.ds(pl.multiple_of(owner * piece + i * 8, 8), 8)
            values = [buf[start + z, place, :] for z in range(layers + 2 * R)]
            for z in range(layers):
                acc = None
                for k in range(KW):
                    term = taps_ref[0, 0, k] * values[z + 2 * R - k if mirror else z + k]
                    acc = term if acc is None else acc + term
                store(z, place, pl.ds(pl.multiple_of(i * 8, 8), 8), acc)
            return carry
        lax.fori_loop(0, piece // 8, tile, 0)

    def store_conv(z, place, local, value):
        conv[z, local, :] = value

    def along_x(value, ref):
        h, l = split(value.reshape(slab * piece, width))
        o = jnp.dot(jnp.concatenate([h, l], 1), ref[...], preferred_element_type=F32)
        return (o[:, :width] + o[:, width:]).reshape(slab, piece, width)

    def along_y(values, ref):
        parts = [split(value) for value in values]
        data = jnp.concatenate(
            [jnp.concatenate([p[0] for p in parts], 1), jnp.concatenate([p[1] for p in parts], 1)], 0)
        o = jnp.dot(ref[...], data, preferred_element_type=F32)
        o = o[:rows] + o[rows:]
        return [o[:, j * width:(j + 1) * width] for j in range(len(values))]

    def ratios(start):
        blurred = along_y([blur[start + j] for j in range(GROUP)], fy)
        ratio = [rec_ref[start + j] / blurred[j] for j in range(GROUP)]
        for j, value in enumerate(along_y(ratio, gy)):
            blur[start + j] = value

    def iteration(t, carry):
        whole[pl.ds(R, slab), at(view)] = own[...]

        def arrive(i, k):
            if not (isinstance(k, int) and k == 0):
                gather(i, k).wait_recv()
            guarded(i, lambda: est_halo(i, k).start())

        def forward(k):
            for i in ORDER:
                guarded(i, lambda: est_halo(i, k).wait_recv())
            owner = peer(k, -1)
            convolve(whole, owner, 0, slab, False, store_conv)
            blur[:, at(owner), :] = along_x(conv[...], fx)

        arrive(first, 0)
        arrive(first, XS)
        if GATHER_BY:
            each(XS + 1, views, lambda k: relay(k).start())
            each(1, XS, lambda k: arrive(first, k))
            each(XS + 1, views, lambda k: arrive(first, k))
        else:
            each(2, views, lambda k: arrive(first, turn(k, 2)))
        arrive(second, 0)

        def arrive_second(k):
            arrive(second, turn(k, 2))

            @pl.when(k == LAG)
            def _():
                forward(0)

            @pl.when(k > LAG)
            def _():
                forward(turn(k - LAG, 2))

        each(1, views, arrive_second)
        each(views - LAG, views, lambda k: forward(turn(k, 2)))

        @pl.when(t == 0)
        def _():
            record.wait()

        for start in range(0, slab, GROUP):
            ratios(start)

        def last_band(k):
            owner = peer(k, 1)
            back[pl.ds(R, slab), at(owner), :] = along_x(blur[:, at(owner), :], gx)
            for i in range(2):
                guarded(i, lambda: back_halo(i, k).start())

        each(1, views, lambda k: last_band(turn(k, 3)))
        last_band(0)

        def sent(k):
            for i in range(2):
                guarded(i, lambda: est_halo(i, k).wait_send())

        each(0, views, sent)
        for i in range(2):
            each(1, views, lambda k: gather(i, k).wait_send())

        for i in ORDER:
            def store_logs(z, place, local, value):
                logs[begin[i] + z, place, :] = flag * jnp.log(value)

            def store_own(z, place, local, value):
                sums[i, 0, z, local, :] = flag * jnp.log(value)

            def backward(k):
                guarded(i, lambda: back_halo(i, k).wait_recv())
                convolve(back, peer(k, 1), begin[i], R, True, store_logs)

            def direct(k):
                backward(k)
                scatter(i, k, k).start()

            def across(k):
                backward(k)
                scatter(i, k, k % XS).start()

            if SCATTER_BY and i == first:
                each(1, views - 1, lambda k: across(turn(k, 3)))
                backward(XS)
            else:
                each(1, views, lambda k: direct(turn(k, 3)))
            guarded(i, lambda: back_halo(i, 0).wait_recv())
            convolve(back, view, begin[i], R, True, store_own)

        if SCATTER_BY:
            each(XS + 1, views, lambda k: scatter(first, k, k).wait_recv())
            place = (pl.ds(begin[first], R), at(peer(XS, 1)))
            passed = logs[place]
            for k in range(XS + 1, views):
                passed = passed + sums[first, k]
            logs[place] = passed
            scatter(first, XS, XS).start()

        for i in ORDER:
            last = XS + 1 if SCATTER_BY and i == first else views
            each(1, last, lambda k: scatter(i, k, k).wait_recv())
            merged = sums[i, 0]
            for k in range(1, last):
                merged = merged + sums[i, k]
            mine = pl.ds(begin[i], R)
            own[mine] = own[mine] * jnp.exp(merged / jnp.full(merged.shape, count, F32))

            @pl.when(t < ITERS - 1)
            def _():
                send_own(i)

        def finished(k):
            for i in range(2):
                guarded(i, lambda: back_halo(i, k).wait_send())

        each(0, views, finished)
        for i in range(2):
            each(1, views, lambda k: scatter(i, k, k).wait_send())
        return carry

    lax.fori_loop(0, ITERS, iteration, 0)
    out_ref[...] = own[...]


def shards(bricks, views, estimate, views_data, psf_taps, view_offsets, coverage):
    slab, piece, width = estimate.shape
    rows = piece * views
    dma = pltpu.SemaphoreType.DMA((2, views))
    return pl.pallas_call(
        functools.partial(kernel, bricks, views),
        out_shape=jax.ShapeDtypeStruct(estimate.shape, F32),
        in_specs=[pl.BlockSpec(memory_space=pltpu.VMEM), pl.BlockSpec(memory_space=pl.ANY)]
        + [pl.BlockSpec(memory_space=pltpu.SMEM)] * 3,
        out_specs=pl.BlockSpec(memory_space=pltpu.VMEM),
        scratch_shapes=[
            pltpu.VMEM((slab, rows, width), F32),
            pltpu.VMEM((slab, piece, width), F32),
            pltpu.VMEM((slab + 2 * R, rows, width), F32),
            pltpu.VMEM((slab, rows, width), F32),
            pltpu.VMEM((slab + 2 * R, rows, width), F32),
            pltpu.VMEM((slab, rows, width), F32),
            pltpu.VMEM((2, views, R, piece, width), F32),
            pltpu.VMEM((slab, piece, width), F32),
        ] + [pltpu.VMEM((2 * rows, 2 * rows), BF16)] * 4 + [dma] * 8 + [pltpu.SemaphoreType.DMA],
        compiler_params=pltpu.CompilerParams(
            collective_id=0, has_side_effects=True, vmem_limit_bytes=40 << 20),
        name="deconvolve",
    )(estimate, views_data, psf_taps, view_offsets, coverage)


def solution(mesh):
    return jax.shard_map(
        functools.partial(shards, mesh.shape["brick"], mesh.shape["view"]),
        mesh=mesh,
        in_specs=(
            P("brick", "view", None),
            P("view", "brick", None, None),
            P("view", None, None),
            P("view", None),
            P("brick", None),
        ),
        out_specs=P("brick", "view", None),
        check_vma=False,
    )
```

time: 723 us -> 167 us (0.23); the launches traced: 714 us -> 166 us
  waiting for transfers between devices: 576 us -> 0 us
  Pallas kernels: 0 us -> 163 us
  matrix products: 45.1 us -> 0 us
  starting transfers between devices: 45 us -> 0 us
  local copies, waits for them, and re-layouts: 18.6 us -> 3.5 us
  other arithmetic: 14.5 us -> 0 us
  between operations: 14.4 us -> 0.01 us
    reduce_scatter x4 -> x0, waiting for transfers between devices: 300 us -> none  [shards(): merged = lax.psum_scatter(weighted, 'view', scatter_dimension=1, tiled=True)]
    all_gather x4 -> x0, waiting for transfers between devices: 212 us -> none  [shards(): whole = lax.all_gather(current, 'view', axis=1, tiled=True)]
    pallas_call x0 -> x1, Pallas kernels: none -> 163 us  [shards(): pl.pallas_call(functools.partial(kernel, bricks, views), out_shape=jax.Sh...]
    ppermute x16 -> x0, waiting for transfers between devices: 64.1 us -> none  [the longest x8 34.9 us: padded_2(): lax.ppermute(lax.slice_in_dim(block, 0, width, axis=dim), axis, backward)]
    dot_general x24 -> x0, matrix products: 45.1 us -> none  [the longest x4 17.5 us: shards(): back = jnp.einsum('ip,pyx->iyx', mirror_z, back_padded, precision=high)]
    ppermute x16 -> x0, starting transfers between devices: 44.7 us -> none  [the longest x8 26.3 us: padded_2(): lax.ppermute(lax.slice_in_dim(block, block.shape[dim] - width, None, axis...]
    concatenate x4 -> x0, local copies, waits for them, and re-layouts: 8.32 us -> none  [padded_2(): block = jnp.concatenate([low, block, high], axis=dim)]
    mul x4 -> x0, other arithmetic: 8.22 us -> none  [shards(): current = current * jnp.exp(merged / count)]
  transfers between devices with their start and end apart: 24 -> 0, of which waited for: 24 -> 0; matrix products, arithmetic and copies ran while one was open for 1% -> 0% of each run, Pallas kernels for 0% -> 0%
where the time goes in v2:
time: 167 us; the launch traced here: 166 us
  Pallas kernels  163 us (98%)
  local copies, waits for them, and re-layouts  3.5 us (2%)
    pallas_call x1, Pallas kernels, shards(): pl.pallas_call(functools.partial(kernel, bricks, views), out_shape=jax.Sh...  163 us
    unnamed x10, local copies, waits for them, and re-layouts  3.5 us

profile of v2, /device:TPU:1, one launch (start us, length us, event | category | flops | bytes accessed | tf_op | source)
XLA Modules:
  0.0 166.3 jit_solution(2530943496090872928)
XLA Ops:
  0.0 0.0 copy-start.3
  0.0 0.0 copy-start.2
  0.0 0.7 copy.6.taps_ref
  0.7 0.0 copy-done.3
  0.7 0.0 copy-done.2
  0.7 0.0 copy-start
  0.7 1.2 copy-done
  1.9 0.0 copy-start.1
  1.9 0.9 copy-done.1
  2.9 162.8 %deconvolve.1 = f32[16,16,128]{2,1,0:T(8,128)S(1)} custom-call(f32[16,16,128]{2,1,0:T(8,128)S(1)} %copy-done.1, f32[1,16,128,128]{3,2,1,0:T(8,128)S(1)} %copy-done, f32[1,3,17]{2,1,0:T(4,128)S(1)} %copy.6.taps_ref, s32[1,2]{1,0:T(1,128)S(1)} %copy-done.2, s32[1,8]{1,0:T(1,128)S(1)} %copy-done.3), custom_call_target="tpu_custom_call" | custom-call | tf_op jit(solution)/shard_map/deconvolve/pallas_call | solution.py:323
  165.7 0.7 copy.8
Async XLA Ops:
  0.0 0.7 copy-start.3
  0.0 0.7 copy-start.2
  0.7 1.2 copy-start
  1.9 0.9 copy-start.1

commit v3 on v2

--- a/solution.py
+++ b/solution.py
@@ -13,9 +13,10 @@
 XS = 4
 ORDER = (0, 1)
 LAG = 5
+EARLY = False
 GATHER_BY = True
-SCATTER_BY = True
-GROUP = 4
+PLAN = ("1d", "1x", "1y", "2d", "2y", "2x", "1p", "1o", "2o")
+GROUP = 16
 MESH = pl.DeviceIdType.MESH
 BF16 = jnp.bfloat16
 F32 = jnp.float32
@@ -27,11 +28,11 @@
 
 
 def kernel(
-    bricks, views, est_ref, rec_hbm, taps_ref, off_ref, cov_ref, out_ref,
+    bricks, views, est_hbm, rec_hbm, taps_ref, off_ref, cov_ref, out_ref,
     rec_ref, own, whole, blur, back, logs, sums, conv, fy, fx, gy, gx,
-    ag_send, ag_recv, est_send, est_recv, back_send, back_recv, rs_send, rs_recv, rec_sem,
+    ag_send, ag_recv, est_send, est_recv, back_send, back_recv, rs_send, rs_recv, est_sem, rec_sem,
 ):
-    slab, piece, width = est_ref.shape
+    slab, piece, width = est_hbm.shape
     rows = piece * views
     brick, view = lax.axis_index("brick"), lax.axis_index("view")
     half = views // XS
@@ -69,9 +70,11 @@
     for i in range(2):
         guarded(i, lambda: greet((beside[i], view)))
 
+    start = pltpu.make_async_copy(est_hbm, own, est_sem)
+    start.start()
     record = pltpu.make_async_copy(rec_hbm.at[0], rec_ref, rec_sem)
     record.start()
-    own[...] = est_ref[...]
+    start.wait()
     pl.semaphore_wait(barrier, views + exists[0].astype(jnp.int32))
 
     def at(owner):
@@ -105,10 +108,11 @@
             device_id=(brick, peer(target, 1)), device_id_type=MESH)
 
     def send_own(i):
+        whole[pl.ds(R + begin[i], R), at(view)] = own[pl.ds(begin[i], R)]
         if GATHER_BY and i == first:
             each(1, XS + 1, lambda k: gather(i, XS + 1 - k).start())
         else:
-            each(1, views, lambda k: gather(i, turn(k, 2)).start())
+            each(1, views, lambda k: gather(i, turn(k, 6)).start())
 
     def turn(k, shift):
         return (k + shift) % (views - 1) + 1
@@ -117,9 +121,9 @@
         send_own(i)
 
     def total(row):
-        value = taps_ref[0, row, 0]
+        value = taps_ref[row, 0, 0]
         for k in range(1, KW):
-            value = value + taps_ref[0, row, k]
+            value = value + taps_ref[row, 0, k]
         return value
 
     def fill(row, offset, scale, lhs, rhs_up, ref):
@@ -128,7 +132,7 @@
         index = (c - r if rhs_up else r - c) + offset + R
         band = jnp.zeros((rows, rows), F32)
         for k in range(KW):
-            band = jnp.where(index == k, taps_ref[0, row, k], band)
+            band = jnp.where(index == k, taps_ref[row, 0, k], band)
         upper, lower = split(band / jnp.full((rows, rows), scale, F32))
         if lhs:
             ref[...] = jnp.concatenate(
@@ -191,13 +195,23 @@
         for j, value in enumerate(along_y(ratio, gy)):
             blur[start + j] = value
 
+    def arrive(i, k):
+        if not (isinstance(k, int) and k == 0):
+            gather(i, k).wait_recv()
+        guarded(i, lambda: est_halo(i, k).start())
+
+    def arrive_across():
+        arrive(first, 0)
+        arrive(first, XS)
+        if GATHER_BY:
+            each(XS + 1, views, lambda k: relay(k).start())
+
+    if EARLY:
+        arrive_across()
+
     def iteration(t, carry):
-        whole[pl.ds(R, slab), at(view)] = own[...]
-
-        def arrive(i, k):
-            if not (isinstance(k, int) and k == 0):
-                gather(i, k).wait_recv()
-            guarded(i, lambda: est_halo(i, k).start())
+        if not EARLY:
+            arrive_across()
 
         def forward(k):
             for i in ORDER:
@@ -206,18 +220,15 @@
             convolve(whole, owner, 0, slab, False, store_conv)
             blur[:, at(owner), :] = along_x(conv[...], fx)
 
-        arrive(first, 0)
-        arrive(first, XS)
         if GATHER_BY:
-            each(XS + 1, views, lambda k: relay(k).start())
             each(1, XS, lambda k: arrive(first, k))
             each(XS + 1, views, lambda k: arrive(first, k))
         else:
-            each(2, views, lambda k: arrive(first, turn(k, 2)))
+            each(2, views, lambda k: arrive(first, turn(k, 6)))
         arrive(second, 0)
 
         def arrive_second(k):
-            arrive(second, turn(k, 2))
+            arrive(second, turn(k, 6))
 
             @pl.when(k == LAG)
             def _():
@@ -225,10 +236,10 @@
 
             @pl.when(k > LAG)
             def _():
-                forward(turn(k - LAG, 2))
+                forward(turn(k - LAG, 6))
 
         each(1, views, arrive_second)
-        each(views - LAG, views, lambda k: forward(turn(k, 2)))
+        each(views - LAG, views, lambda k: forward(turn(k, 6)))
 
         @pl.when(t == 0)
         def _():
@@ -243,7 +254,8 @@
             for i in range(2):
                 guarded(i, lambda: back_halo(i, k).start())
 
-        each(1, views, lambda k: last_band(turn(k, 3)))
+        for k in (5, 6, 7, 1, 2, 3, 4):
+            last_band(k)
         last_band(0)
 
         def sent(k):
@@ -254,34 +266,25 @@
         for i in range(2):
             each(1, views, lambda k: gather(i, k).wait_send())
 
-        for i in ORDER:
+        def backward(i, k, own_piece):
             def store_logs(z, place, local, value):
                 logs[begin[i] + z, place, :] = flag * jnp.log(value)
 
             def store_own(z, place, local, value):
                 sums[i, 0, z, local, :] = flag * jnp.log(value)
 
-            def backward(k):
-                guarded(i, lambda: back_halo(i, k).wait_recv())
-                convolve(back, peer(k, 1), begin[i], R, True, store_logs)
-
-            def direct(k):
-                backward(k)
-                scatter(i, k, k).start()
-
-            def across(k):
-                backward(k)
-                scatter(i, k, k % XS).start()
-
-            if SCATTER_BY and i == first:
-                each(1, views - 1, lambda k: across(turn(k, 3)))
-                backward(XS)
-            else:
-                each(1, views, lambda k: direct(turn(k, 3)))
-            guarded(i, lambda: back_halo(i, 0).wait_recv())
-            convolve(back, view, begin[i], R, True, store_own)
-
-        if SCATTER_BY:
+            guarded(i, lambda: back_halo(i, k).wait_recv())
+            convolve(back, peer(k, 1), begin[i], R, True, store_own if own_piece else store_logs)
+
+        def direct(i, k):
+            backward(i, k, False)
+            scatter(i, k, k).start()
+
+        def across(k):
+            backward(first, k, False)
+            scatter(first, k, k % XS).start()
+
+        def pass_on():
             each(XS + 1, views, lambda k: scatter(first, k, k).wait_recv())
             place = (pl.ds(begin[first], R), at(peer(XS, 1)))
             passed = logs[place]
@@ -290,8 +293,24 @@
             logs[place] = passed
             scatter(first, XS, XS).start()
 
+        for step in PLAN:
+            step_class = first if step[0] == "1" else second
+            run = across if step[0] == "1" else functools.partial(direct, second)
+            if step[1] == "x":
+                each(1, XS, run)
+            elif step[1] == "d":
+                each(XS + 1, views, run)
+            elif step[1] == "y" and step[0] == "1":
+                backward(first, XS, False)
+            elif step[1] == "y":
+                run(XS)
+            elif step[1] == "o":
+                backward(step_class, 0, True)
+            else:
+                pass_on()
+
         for i in ORDER:
-            last = XS + 1 if SCATTER_BY and i == first else views
+            last = XS + 1 if i == first else views
             each(1, last, lambda k: scatter(i, k, k).wait_recv())
             merged = sums[i, 0]
             for k in range(1, last):
@@ -302,6 +321,8 @@
             @pl.when(t < ITERS - 1)
             def _():
                 send_own(i)
+                if EARLY and i == first:
+                    arrive_across()
 
         def finished(k):
             for i in range(2):
@@ -323,7 +344,7 @@
     return pl.pallas_call(
         functools.partial(kernel, bricks, views),
         out_shape=jax.ShapeDtypeStruct(estimate.shape, F32),
-        in_specs=[pl.BlockSpec(memory_space=pltpu.VMEM), pl.BlockSpec(memory_space=pl.ANY)]
+        in_specs=[pl.BlockSpec(memory_space=pl.ANY)] * 2
         + [pl.BlockSpec(memory_space=pltpu.SMEM)] * 3,
         out_specs=pl.BlockSpec(memory_space=pltpu.VMEM),
         scratch_shapes=[
@@ -335,11 +356,11 @@
             pltpu.VMEM((slab, rows, width), F32),
             pltpu.VMEM((2, views, R, piece, width), F32),
             pltpu.VMEM((slab, piece, width), F32),
-        ] + [pltpu.VMEM((2 * rows, 2 * rows), BF16)] * 4 + [dma] * 8 + [pltpu.SemaphoreType.DMA],
+        ] + [pltpu.VMEM((2 * rows, 2 * rows), BF16)] * 4 + [dma] * 8 + [pltpu.SemaphoreType.DMA] * 2,
         compiler_params=pltpu.CompilerParams(
-            collective_id=0, has_side_effects=True, vmem_limit_bytes=40 << 20),
+            collective_id=0, has_side_effects=True, vmem_limit_bytes=60 << 20),
         name="deconvolve",
-    )(estimate, views_data, psf_taps, view_offsets, coverage)
+    )(estimate, views_data, jnp.transpose(psf_taps, (1, 0, 2)), view_offsets, coverage)
 
 
 def solution(mesh):

time: 167 us -> 158 us (0.946)
  Pallas kernels: 163 us -> 156 us
  local copies, waits for them, and re-layouts: 3.5 us -> 1.57 us
    pallas_call x1, Pallas kernels: 163 us -> 156 us  [shards(): pl.pallas_call(functools.partial(kernel, bricks, views), out_shape=jax.Sh...]
    unnamed x10 -> x1, local copies, waits for them, and re-layouts: 3.5 us -> 1.57 us
where the time goes in v3:
time: 158 us
  Pallas kernels  156 us (99%)
    pallas_call x1, Pallas kernels, shards(): pl.pallas_call(functools.partial(kernel, bricks, views), out_shape=jax.Sh...  156 us

profile of v3, /device:TPU:1, one launch (start us, length us, event | category | flops | bytes accessed | tf_op | source)
XLA Modules:
  0.0 157.8 jit_solution(2310059758249704627)
XLA Ops:
  0.0 156.2 %deconvolve.1 = f32[16,16,128]{2,1,0:T(8,128)} custom-call(f32[16,16,128]{2,1,0:T(8,128)} %est_hbm.1, f32[1,16,128,128]{3,2,1,0:T(8,128)} %rec_hbm.1, f32[3,1,17]{2,1,0:T(1,128)} %bitcast.1, s32[1,2]{1,0:T(1,128)} %off_ref.1, s32[1,8]{1,0:T(1,128)} %cov_ref.1), custom_call_target="tpu_custom_call" | custom-call | tf_op jit(solution)/shard_map/deconvolve/pallas_call | solution.py:344
  156.2 1.6 copy.7

commit v4 on v3

--- a/solution.py
+++ b/solution.py
@@ -112,10 +112,10 @@
         if GATHER_BY and i == first:
             each(1, XS + 1, lambda k: gather(i, XS + 1 - k).start())
         else:
-            each(1, views, lambda k: gather(i, turn(k, 6)).start())
-
-    def turn(k, shift):
-        return (k + shift) % (views - 1) + 1
+            each(1, views, lambda k: gather(i, turn(k)).start())
+
+    def turn(k):
+        return (XS * k - 1) % (views - 1) + 1
 
     for i in ORDER:
         send_own(i)
@@ -169,9 +169,10 @@
                 for k in range(KW):
                     term = taps_ref[0, 0, k] * values[z + 2 * R - k if mirror else z + k]
                     acc = term if acc is None else acc + term
-                store(z, place, pl.ds(pl.multiple_of(i * 8, 8), 8), acc)
+                store(z, place, pl.ds(i * 8, 8), acc)
             return carry
-        lax.fori_loop(0, piece // 8, tile, 0)
+        for i in range(piece // 8):
+            tile(i, 0)
 
     def store_conv(z, place, local, value):
         conv[z, local, :] = value
@@ -224,11 +225,11 @@
             each(1, XS, lambda k: arrive(first, k))
             each(XS + 1, views, lambda k: arrive(first, k))
         else:
-            each(2, views, lambda k: arrive(first, turn(k, 6)))
+            each(2, views, lambda k: arrive(first, turn(k)))
         arrive(second, 0)
 
         def arrive_second(k):
-            arrive(second, turn(k, 6))
+            arrive(second, turn(k))
 
             @pl.when(k == LAG)
             def _():
@@ -236,10 +237,10 @@
 
             @pl.when(k > LAG)
             def _():
-                forward(turn(k - LAG, 6))
+                forward(turn(k - LAG))
 
         each(1, views, arrive_second)
-        each(views - LAG, views, lambda k: forward(turn(k, 6)))
+        each(views - LAG, views, lambda k: forward(turn(k)))
 
         @pl.when(t == 0)
         def _():

time: 158 us -> 156 us (0.987)
  Pallas kernels: 156 us -> 154 us
    pallas_call x1, Pallas kernels: 156 us -> 154 us  [shards(): pl.pallas_call(functools.partial(kernel, bricks, views), out_shape=jax.Sh...]
where the time goes in v4:
time: 156 us
  Pallas kernels  154 us (99%)
  local copies, waits for them, and re-layouts  1.57 us (1%)
    pallas_call x1, Pallas kernels, shards(): pl.pallas_call(functools.partial(kernel, bricks, views), out_shape=jax.Sh...  154 us

profile of v4, /device:TPU:1, one launch (start us, length us, event | category | flops | bytes accessed | tf_op | source)
XLA Modules:
  0.0 156.1 jit_solution(6453615792805125636)
XLA Ops:
  0.0 154.5 %deconvolve.1 = f32[16,16,128]{2,1,0:T(8,128)} custom-call(f32[16,16,128]{2,1,0:T(8,128)} %est_hbm.1, f32[1,16,128,128]{3,2,1,0:T(8,128)} %rec_hbm.1, f32[3,1,17]{2,1,0:T(1,128)} %bitcast.1, s32[1,2]{1,0:T(1,128)} %off_ref.1, s32[1,8]{1,0:T(1,128)} %cov_ref.1), custom_call_target="tpu_custom_call" | custom-call | tf_op jit(solution)/shard_map/deconvolve/pallas_call | solution.py:345
  154.5 1.6 %copy.7 = f32[16,16,128]{2,1,0:T(8,128)} copy(f32[16,16,128]{2,1,0:T(8,128)} %deconvolve.1) | data formatting | bytes 262144
